TPU v7x, 32 devices: a whole 2x2x4 slice. The times are simulated.
32 devices in a mesh: dp: 8 (over y, x, core), expert: 4 (over z).
Axes of the slice: x: 2, y: 2, z: 4, core: 2. Of those that a mesh axis runs over, the one named last changes fastest.
Arguments:
- tokens: bfloat16 [4096, 2048], P(('dp', 'expert')), may hold values from -6 to 6
- routes: int32 [4096, 1], P(('dp', 'expert')), may hold values from 0 to 3; in each aligned block of 128 rows (0 to 127, 128 to 255, ...) at most 40 rows name the same one
- route_gates: float32 [4096, 1], P(('dp', 'expert')), may hold values from 0.1 to 1
- w_gate: bfloat16 [4, 2048, 384], P('expert'), may hold values from -0.125 to 0.125
- w_up: bfloat16 [4, 2048, 384], P('expert'), may hold values from -0.125 to 0.125
- w_down: bfloat16 [4, 384, 2048], P('expert'), may hold values from -0.3125 to 0.3125
- cotangent: bfloat16 [4096, 2048], P(('dp', 'expert')), may hold values from -6 to 6
Outputs:
- mixed: bfloat16 [4096, 2048], P(('dp', 'expert'))
- d_tokens: bfloat16 [4096, 2048], P(('dp', 'expert'))
- d_gates: float32 [4096, 1], P(('dp', 'expert'))
- d_w_down: bfloat16 [4, 384, 2048], P('expert', 'dp')
Inputs may be any that keep to these rules, and one draw needn't show every extreme that they name: `routes`: each token names exactly one expert. Among the rows of one device no expert is named more than 40 times, a bound that some block reaches in some devices' rows; every expert is named somewhere.
All inputs are finite; a program needn't handle non-finite values.
Results may differ from a plain program's by a relative error of at most 0.0058.
Values may be sent and summed in bfloat16 or wider, within the bound.
A program may use at most 64 MiB of HBM per device.

v0:
```python
import math

import jax
import jax.numpy as jnp
from jax import lax
from jax.sharding import PartitionSpec as P


def send_back(values):
    return lax.all_to_all(values, "expert", split_axis=0, concat_axis=0, tiled=True)


def per_device(tokens, routes, route_gates, w_gate, w_up, w_down, cotangent):
    tok_rows, model_width = tokens.shape
    route_count = routes.shape[1]
    expert_count = w_gate.shape[0] * lax.axis_size("expert")
    capacity = 5 * tok_rows * route_count // (4 * expert_count)
    slot_count = expert_count * capacity
    flattened = routes.reshape(-1)
    route_rows = flattened.shape[0]
    one_hot = (flattened[:, None] == jnp.arange(expert_count, dtype=jnp.int32)[None, :]).astype(
        jnp.int32
    )
    earlier = jnp.cumsum(one_hot, axis=0) - one_hot
    slot_of = jnp.sum(earlier * one_hot, axis=1)
    target = flattened * capacity + slot_of
    source_row = (
        jnp.zeros((slot_count,), jnp.int32).at[target].set(jnp.arange(route_rows, dtype=jnp.int32))
    )
    filled = jnp.zeros((slot_count,), jnp.bool_).at[target].set(True)
    outgoing = jnp.where(
        filled[:, None], tokens[source_row // route_count], jnp.zeros((), tokens.dtype)
    )
    outgoing = outgoing.reshape(expert_count, capacity, model_width)
    gate_matrix = w_gate[0]
    up_matrix = w_up[0]
    down_matrix = w_down[0]
    arrived = lax.all_to_all(outgoing, "expert", split_axis=0, concat_axis=0, tiled=True)
    project_pre_gate = jnp.einsum(
        "scd,df->scf", arrived, gate_matrix, preferred_element_type=jnp.float32
    )
    project_pre_up = jnp.einsum(
        "scd,df->scf", arrived, up_matrix, preferred_element_type=jnp.float32
    )
    hidden = (project_pre_gate * jax.nn.sigmoid(project_pre_gate) * project_pre_up).astype(
        jnp.bfloat16
    )
    expert_out = jnp.einsum(
        "scf,fd->scd", hidden, down_matrix, preferred_element_type=jnp.float32
    ).astype(jnp.bfloat16)
    hidden, returned = (hidden, send_back(expert_out))
    results = (returned, project_pre_gate, project_pre_up, hidden)
    returned = results[0]
    hidden = results[-1]
    out_rows = returned.reshape(slot_count, model_width)[target].reshape(
        tok_rows, route_count, model_width
    )
    mixed = jnp.sum(route_gates[:, :, None] * out_rows.astype(jnp.float32), axis=1).astype(
        jnp.bfloat16
    )
    d_gates = jnp.einsum("td,tkd->tk", cotangent, out_rows, preferred_element_type=jnp.float32)
    weighted = (route_gates[:, :, None] * cotangent[:, None, :].astype(jnp.float32)).astype(
        jnp.bfloat16
    )
    weighted = weighted.reshape(route_rows, model_width)
    grad_send = jnp.where(filled[:, None], weighted[source_row], jnp.zeros((), weighted.dtype))
    grad_send = grad_send.reshape(expert_count, capacity, model_width)
    grad_arrived = lax.all_to_all(grad_send, "expert", split_axis=0, concat_axis=0, tiled=True)
    pre_gate = results[1]
    pre_up = results[2]
    grad_scale = 1.0 / math.sqrt(route_count * tok_rows * lax.axis_size("dp"))
    hidden_rows = hidden.reshape(slot_count, hidden.shape[2])
    grad_rows = grad_arrived.reshape(slot_count, model_width)
    grad_hidden = jnp.einsum(
        "scd,fd->scf", grad_arrived, down_matrix, preferred_element_type=jnp.float32
    )
    sigmoid_gate = jax.nn.sigmoid(pre_gate)
    grad_gate = (
        grad_hidden * pre_up * sigmoid_gate * (1.0 + pre_gate * (1.0 - sigmoid_gate))
    ).astype(jnp.bfloat16)
    grad_up = (grad_hidden * pre_gate * sigmoid_gate).astype(jnp.bfloat16)
    grad_input = jnp.einsum(
        "scf,df->scd", grad_gate, gate_matrix, preferred_element_type=jnp.float32
    ) + jnp.einsum("scf,df->scd", grad_up, up_matrix, preferred_element_type=jnp.float32)
    grad_returned = lax.all_to_all(
        grad_input.astype(jnp.bfloat16), "expert", split_axis=0, concat_axis=0, tiled=True
    )
    product = lax.dot_general(
        hidden_rows, grad_rows, (((0,), (0,)), ((), ())), preferred_element_type=jnp.float32
    )
    down_rows = lax.psum_scatter(product * grad_scale, "dp", scatter_dimension=0, tiled=True)
    input_rows = grad_returned.reshape(slot_count, model_width)[target]
    input_rows = input_rows.reshape(tok_rows, route_count, model_width)
    d_tokens = jnp.sum(input_rows.astype(jnp.float32), axis=1).astype(jnp.bfloat16)
    d_w_down = down_rows.astype(jnp.bfloat16)[None]
    return (mixed, d_tokens, d_gates, d_w_down)


def solution(mesh):
    in_specs = (
        P(("dp", "expert"), None),
        P(("dp", "expert"), None),
        P(("dp", "expert"), None),
        P("expert", None, None),
        P("expert", None, None),
        P("expert", None, None),
        P(("dp", "expert"), None),
    )
    out_specs = (
        P(("dp", "expert"), None),
        P(("dp", "expert"), None),
        P(("dp", "expert"), None),
        P("expert", "dp", None),
    )
    return jax.shard_map(
        per_device, mesh=mesh, in_specs=in_specs, out_specs=out_specs, check_vma=False
    )
```

profile of v0, /device:TPU:8, one launch (start us, length us, event | category | flops | bytes accessed | tf_op | source)
XLA Modules:
  0.0 141.6 jit_solution(17287730674799018943)
XLA Ops:
  7.2 0.9 fusion.16
  8.2 0.8 select_reduce_fusion
  9.7 1.0 scatter_custom_fusion
  10.8 1.0 scatter_custom_fusion.1
  11.8 2.8 %gather_fusion = bf16[160,2048]{1,0:T(8,128)(2,1)S(1)} fusion(bf16[128,2048]{1,0:T(8,128)(2,1)} %param.7, s32[1024]{0:T(1024)S(1)} %pad_clamp_fusion.1), kind=kCustom, calls=%fused_computation | custom fusion | bytes 1311360 | tf_op jit(solution)/shard_map/gather | solution.py:32
  14.8 20.7 %all_to_all.20 = bf16[4,40,2048]{2,1,0:T(8,128)(2,1)S(1)} all-to-all(bf16[4,40,2048]{2,1,0:T(8,128)(2,1)S(1)} %broadcast_select_fusion.1), channel_id=1, replica_groups=mesh['dp'=8,'expert'=4] {'expert'}, dimensions={0} | all-to-all | bytes 1310720 | tf_op jit(solution)/shard_map/all_to_all | solution.py:38
  36.0 1.2 multiply_convert_fusion.2
  37.9 1.4 convolution_convert_fusion
  39.2 5.3 %all-to-all-start.1 = ((bf16[4,40,2048]{2,1,0:T(8,128)(2,1)}), bf16[4,40,2048]{2,1,0:T(8,128)(2,1)S(1)}, u32[]{:S(2)}, u32[]{:S(2)}) async-start(bf16[4,40,2048]{2,1,0:T(8,128)(2,1)} %convolution_convert_fusion), calls=%async_computation.1 | async-start | bytes 1310720 | tf_op jit(solution)/shard_map/all_to_all | solution.py:10
  44.5 13.2 %all-to-all-done.1 = bf16[4,40,2048]{2,1,0:T(8,128)(2,1)S(1)} async-done(((bf16[4,40,2048]{2,1,0:T(8,128)(2,1)}), bf16[4,40,2048]{2,1,0:T(8,128)(2,1)S(1)}, u32[]{:S(2)}, u32[]{:S(2)}) %all-to-all-start.1) | async-done | bytes 655392 | tf_op jit(solution)/shard_map/all_to_all | solution.py:10
  57.7 0.9 gather_fusion.1
  58.6 2.7 %fusion.13 = (f32[128]{0:T(128)}, bf16[128,2048]{1,0:T(8,128)(2,1)}, bf16[128,2048]{1,0:T(8,128)(2,1)S(1)}) fusion(bf16[128,2048]{1,0:T(8,128)(2,1)} %param.13, bf16[128,2048]{1,0:T(8,128)(2,1)S(1)} %gather_fusion.1, f32[128]{0:T(128)S(1)} %bitcast.51), kind=kLoop, calls=%fused_computation.25 | loop fusion | flops 2097024 | bytes 2098176 | tf_op jit(solution)/shard_map/td,tkd->tk/dot_general | solution.py:61
  61.3 1.0 gather_fusion.2
  62.5 20.7 %all_to_all.21 = bf16[4,40,2048]{2,1,0:T(8,128)(2,1)S(1)} all-to-all(bf16[4,40,2048]{2,1,0:T(8,128)(2,1)S(1)} %broadcast_select_fusion), channel_id=1, replica_groups=mesh['dp'=8,'expert'=4] {'expert'}, dimensions={0} | all-to-all | bytes 1310720 | tf_op jit(solution)/shard_map/all_to_all | solution.py:68
  83.1 0.8 copy-done.5
  84.0 2.3 %bitcast_multiply_fusion = f32[384,2048]{1,0:T(8,128)} fusion(bf16[4,40,384]{2,1,0:T(8,128)(2,1)S(1)} %copy-done.8, bf16[4,40,2048]{2,1,0:T(8,128)(2,1)S(1)} %all_to_all.21), kind=kOutput, calls=%fused_computation.6 | convolution fusion | flops 252444672 | bytes 3923968 | tf_op jit(solution)/shard_map/dot_general | solution.py:88
  86.3 1.4 copy-done.2
  87.6 1.9 %fusion.1 = f32[4,40,384]{2,1,0:T(8,128)S(1)} fusion(bf16[4,40,2048]{2,1,0:T(8,128)(2,1)} %copy-done.5, bf16[1,384,2048]{2,1,0:T(8,128)(2,1)S(1)} %copy-done.2), kind=kOutput, calls=%fused_computation.10 | convolution fusion | flops 251658240 | bytes 2473984 | tf_op jit(solution)/shard_map/scd,fd->scf/dot_general | solution.py:74
  89.5 0.8 fusion.7
  90.4 0.9 fusion
  91.2 19.3 %all_to_all.22 = bf16[4,40,2048]{2,1,0:T(8,128)(2,1)S(1)} all-to-all(bf16[4,40,2048]{2,1,0:T(8,128)(2,1)S(1)} %fusion), channel_id=1, replica_groups=mesh['dp'=8,'expert'=4] {'expert'}, dimensions={0} | all-to-all | bytes 1310720 | tf_op jit(solution)/shard_map/all_to_all | solution.py:85
  110.6 1.7 %gather_fusion.3 = bf16[128,2048]{1,0:T(8,128)(2,1)} fusion(bf16[160,2048]{1,0:T(8,128)(2,1)S(1)} %bitcast.46, s32[1024]{0:T(1024)S(1)} %pad_clamp_fusion), kind=kCustom, calls=%fused_computation.3 | custom fusion | bytes 1049088 | tf_op jit(solution)/shard_map/gather | solution.py:92
  112.3 20.7 %reduce-scatter.2.cloned.1.call-done = f32[48,2048]{1,0:T(8,128)} async-done(((f32[384,2048]{1,0:T(8,128)}), f32[48,2048]{1,0:T(8,128)}) %reduce-scatter.2.cloned.1.call-update) | async-done | bytes 393232 | tf_op jit(solution)/shard_map/reduce_scatter | solution.py:91
  133.0 1.7 %convert_bitcast_fusion = bf16[1,48,2048]{2,1,0:T(8,128)(2,1)} fusion(f32[48,2048]{1,0:T(8,128)} %reduce-scatter.2.cloned.1.call-done), kind=kLoop, calls=%fused_computation.32 | loop fusion | flops 98304 | bytes 589824 | tf_op jit(solution)/shard_map/broadcast_in_dim | solution.py:95
  (31 shorter events, 2.4 us)
Async XLA Ops:
  7.2 28.8 %copy-start = (bf16[1,2048,384]{2,1,0:T(8,128)(2,1)S(1)}, bf16[1,2048,384]{2,1,0:T(8,128)(2,1)}, u32[]{:S(2)}) copy-start(bf16[1,2048,384]{2,1,0:T(8,128)(2,1)} %param.11) | copy-start | bytes 4718596
  14.6 20.9 %copy-start.3 = (bf16[1,2048,384]{2,1,0:T(8,128)(2,1)S(1)}, bf16[1,2048,384]{2,1,0:T(8,128)(2,1)}, u32[]{:S(2)}) copy-start(bf16[1,2048,384]{2,1,0:T(8,128)(2,1)} %param.10) | copy-start | bytes 4718596
  36.0 1.9 %copy-start.1 = (bf16[1,384,2048]{2,1,0:T(8,128)(2,1)S(1)}, bf16[1,384,2048]{2,1,0:T(8,128)(2,1)}, u32[]{:S(2)}) copy-start(bf16[1,384,2048]{2,1,0:T(8,128)(2,1)} %param.12) | copy-start | bytes 4718596
  37.2 0.6 copy-start.7
  39.2 18.4 %all-to-all-start.1 = ((bf16[4,40,2048]{2,1,0:T(8,128)(2,1)}), bf16[4,40,2048]{2,1,0:T(8,128)(2,1)S(1)}, u32[]{:S(2)}, u32[]{:S(2)}) async-start(bf16[4,40,2048]{2,1,0:T(8,128)(2,1)} %convolution_convert_fusion), calls=%async_computation.1 | async-start | bytes 1310720 | tf_op jit(solution)/shard_map/all_to_all | solution.py:10
  44.5 88.5 %reduce-scatter.2.cloned.1.call-start = ((), (), s32[]{:S(2)}) async-start(), calls=%async_computation.5 | async-start | bytes 3538944 | tf_op jit(solution)/shard_map/reduce_scatter | solution.py:91
  57.7 0.9 copy-start.9
  62.3 21.6 %copy-start.8 = (bf16[4,40,384]{2,1,0:T(8,128)(2,1)S(1)}, bf16[4,40,384]{2,1,0:T(8,128)(2,1)}, u32[]{:S(2)}) copy-start(bf16[4,40,384]{2,1,0:T(8,128)(2,1)} %copy-done.7) | copy-start | bytes 368644
  83.1 0.8 copy-start.5
  86.2 1.4 copy-start.2
  87.6 1.9 %copy-start.4 = (bf16[1,2048,384]{2,1,0:T(8,128)(2,1)S(1)}, bf16[1,2048,384]{2,1,0:T(8,128)(2,1)}, u32[]{:S(2)}) copy-start(bf16[1,2048,384]{2,1,0:T(8,128)(2,1)} %param.10) | copy-start | bytes 4718596
  87.6 1.9 %copy-start.6 = (f32[4,40,384]{2,1,0:T(8,128)S(1)}, f32[4,40,384]{2,1,0:T(8,128)}, u32[]{:S(2)}) copy-start(f32[4,40,384]{2,1,0:T(8,128)} %get-tuple-element.8) | copy-start | bytes 737284
Sparse Core Ops, SparseCore 0:
  86.4 46.6 reduce-scatter.1
where the time goes:
time: 144 us; the launch traced here: 142 us
  blocking collectives  60.7 us (42%)
  waiting for transfers between devices  33.9 us (24%)
  between operations  14.2 us (10%)
  local copies, waits for them, and re-layouts  11.5 us (8%)
  matrix products  8.87 us (6%)
  other arithmetic  7.14 us (5%)
  starting transfers between devices  5.26 us (4%)
    all_to_all x1, blocking collectives, per_device(): lax.all_to_all(outgoing, 'expert', split_axis=0, concat_axis=0, tiled=True)  20.7 us
    reduce_scatter x1, waiting for transfers between devices, per_device(): lax.psum_scatter(product * grad_scale, 'dp', scatter_dimension=0, tiled=T...  20.7 us
    all_to_all x1, blocking collectives, per_device(): lax.all_to_all(grad_send, 'expert', split_axis=0, concat_axis=0, tiled=True)  20.7 us
    all_to_all x1, blocking collectives, per_device(): lax.all_to_all(grad_input.astype(jnp.bfloat16), 'expert', split_axis=0, c...  19.3 us
    all_to_all x1, waiting for transfers between devices, send_back(): lax.all_to_all(values, 'expert', split_axis=0, concat_axis=0, tiled=True)  13.2 us
    all_to_all x1, starting transfers between devices, send_back(): lax.all_to_all(values, 'expert', split_axis=0, concat_axis=0, tiled=True)  5.26 us
    unnamed x20, local copies, waits for them, and re-layouts  2.9 us
  transfers between devices with their start and end apart: 2, of which 2 were waited for; matrix products, arithmetic and copies ran while one was open for 4% of the time, Pallas kernels for 0%

commit v1 on v0

v1 whole, which is shorter than its diff:
```python
import functools
import math

import jax
import jax.numpy as jnp
from jax import lax
from jax.experimental import pallas as pl
from jax.experimental.pallas import tpu as pltpu
from jax.sharding import PartitionSpec as P

MESH = pl.DeviceIdType.MESH
F32 = jnp.float32
BF16 = jnp.bfloat16
ROWS = (((1,), (0,)), ((), ()))
BOTH_LAST = (((1,), (1,)), ((), ()))
BOTH_FIRST = (((0,), (0,)), ((), ()))
X, G, OUT, GI = range(4)


def dot(a, b, dims=ROWS):
    return lax.dot_general(a, b, dims, preferred_element_type=F32)


def joined(ref, count):
    return jnp.concatenate([ref[e].astype(F32) for e in range(count)], axis=0).astype(BF16)


def kernel(
    n, n_dp, cap, scale,
    tokens, routes, gates, w_gate_hbm, w_up_hbm, w_down_hbm, cotangent,
    mixed, d_tokens, d_gates, d_w_down,
    x_send, g_send, out_send, gi_send, x_recv, g_recv, out_recv, gi_recv,
    part_send, part_recv, w_gate, w_up, w_down, weighted,
    send_sem, recv_sem, part_send_sem, part_recv_sem, weight_sem,
):
    me = lax.axis_index("expert")
    my_dp = lax.axis_index("dp")
    t = tokens.shape[0]

    weight_copies = [
        pltpu.make_async_copy(src.at[0], dst, weight_sem.at[i])
        for i, (src, dst) in enumerate(
            ((w_gate_hbm, w_gate), (w_up_hbm, w_up), (w_down_hbm, w_down))
        )
    ]
    for copy in weight_copies:
        copy.start()

    barrier = pltpu.get_barrier_semaphore()
    for k in range(1, n):
        pl.semaphore_signal(
            barrier, inc=1, device_id={"expert": lax.rem(me + k, n)}, device_id_type=MESH
        )
    for k in range(1, n_dp):
        pl.semaphore_signal(
            barrier, inc=1, device_id={"dp": lax.rem(my_dp + k, n_dp)}, device_id_type=MESH
        )

    row = routes[...].astype(F32)
    first = lax.broadcasted_iota(jnp.int32, (t, t), 0)
    second = lax.broadcasted_iota(jnp.int32, (t, t), 1)
    eye = first == second
    column = jnp.sum(jnp.where(eye, row, 0.0), axis=1, keepdims=True)
    same = column == row
    target_row = row * cap + jnp.sum(
        jnp.where(same & (first < second), 1.0, 0.0), axis=0, keepdims=True
    )
    target_column = column * cap + jnp.sum(
        jnp.where(same & (second < first), 1.0, 0.0), axis=1, keepdims=True
    )
    gate_column = jnp.sum(jnp.where(eye, gates[...], 0.0), axis=1, keepdims=True)
    slot = lax.broadcasted_iota(jnp.int32, (cap, t), 0)

    def pick(expert):
        return jnp.where((slot + expert * cap).astype(F32) == target_row, 1.0, 0.0).astype(BF16)

    def exchange(kind, k, source, landing):
        return pltpu.make_async_remote_copy(
            src_ref=source,
            dst_ref=landing.at[me],
            send_sem=send_sem.at[kind, k],
            recv_sem=recv_sem.at[kind, k],
            device_id={"expert": lax.rem(me + k, n)},
            device_id_type=MESH,
        )

    picks = [pick(lax.rem(me + k, n)) for k in range(n)]
    sends = [[], [], [], []]
    for k in range(1, n):
        x_send[k] = dot(picks[k], tokens[...]).astype(BF16)
        if k == 1:
            pl.semaphore_wait(barrier, n + n_dp - 2)
        sends[X].append(exchange(X, k, x_send.at[k], x_recv))
        sends[X][-1].start()
    weighted[...] = (gate_column * cotangent[...].astype(F32)).astype(BF16)
    for k in range(1, n):
        g_send[k] = dot(picks[k], weighted[...]).astype(BF16)
        sends[G].append(exchange(G, k, g_send.at[k], g_recv))
        sends[G][-1].start()
    x_recv[me] = dot(picks[0], tokens[...]).astype(BF16)
    g_recv[me] = dot(picks[0], weighted[...]).astype(BF16)

    for copy in weight_copies:
        copy.wait()
    for copy in sends[X]:
        copy.wait_recv()
    x = joined(x_recv, n)
    pre_gate = dot(x, w_gate[...])
    pre_up = dot(x, w_up[...])
    sigmoid = jax.nn.sigmoid(pre_gate)
    hidden = (pre_gate * sigmoid * pre_up).astype(BF16)
    out = dot(hidden, w_down[...])
    for e in range(n):
        out_send[e] = out[e * cap : (e + 1) * cap].astype(BF16)
    for k in range(1, n):
        sends[OUT].append(exchange(OUT, k, out_send.at[lax.rem(me + k, n)], out_recv))
        sends[OUT][-1].start()
    out_recv[me] = out_send[me]

    for copy in sends[G]:
        copy.wait_recv()
    g = joined(g_recv, n)
    grad_hidden = dot(g, w_down[...], BOTH_LAST)
    grad_gate = (grad_hidden * pre_up * sigmoid * (1.0 + pre_gate * (1.0 - sigmoid))).astype(BF16)
    grad_up = (grad_hidden * pre_gate * sigmoid).astype(BF16)
    grad_in = dot(grad_gate, w_gate[...], BOTH_LAST) + dot(grad_up, w_up[...], BOTH_LAST)
    for e in range(n):
        gi_send[e] = grad_in[e * cap : (e + 1) * cap].astype(BF16)
    for k in range(1, n):
        sends[GI].append(exchange(GI, k, gi_send.at[lax.rem(me + k, n)], gi_recv))
        sends[GI][-1].start()
    gi_recv[me] = gi_send[me]

    product = dot(hidden, g, BOTH_FIRST) * scale
    part_rows = product.shape[0] // n_dp
    for j in range(n_dp):
        part_send[j] = product[j * part_rows : (j + 1) * part_rows].astype(BF16)
    parts = []
    for k in range(1, n_dp):
        peer = lax.rem(my_dp + k, n_dp)
        parts.append(
            pltpu.make_async_remote_copy(
                src_ref=part_send.at[peer],
                dst_ref=part_recv.at[k],
                send_sem=part_send_sem.at[k],
                recv_sem=part_recv_sem.at[k],
                device_id={"dp": peer},
                device_id_type=MESH,
            )
        )
        parts[-1].start()

    spread = jnp.where(
        lax.broadcasted_iota(jnp.int32, (t, n * cap), 1).astype(F32) == target_column, 1.0, 0.0
    ).astype(BF16)
    for copy in sends[OUT]:
        copy.wait_recv()
    rows = dot(spread, joined(out_recv, n))
    mixed[...] = (gate_column * rows).astype(BF16)
    inner = jnp.sum(cotangent[...].astype(F32) * rows, axis=1, keepdims=True)
    d_gates[...] = jnp.sum(jnp.where(eye, inner, 0.0), axis=0, keepdims=True)

    total = part_send[my_dp].astype(F32)
    for k, copy in enumerate(parts, 1):
        copy.wait_recv()
        total = total + part_recv[k].astype(F32)
    d_w_down[0] = total.astype(BF16)

    for copy in sends[GI]:
        copy.wait_recv()
    d_tokens[...] = dot(spread, joined(gi_recv, n)).astype(BF16)
    for copies in (*sends, parts):
        for copy in copies:
            copy.wait_send()


def per_device(n, n_dp, tokens, routes, route_gates, w_gate, w_up, w_down, cotangent):
    t, d = tokens.shape
    ff = w_down.shape[1]
    cap = 5 * t // (4 * n)
    cap = -(-cap // 8) * 8
    scale = 1.0 / math.sqrt(routes.shape[1] * t * n_dp)
    vmem = pl.BlockSpec(memory_space=pltpu.VMEM)
    hbm = pl.BlockSpec(memory_space=pl.ANY)
    block = pltpu.VMEM((n, cap, d), BF16)
    part = pltpu.VMEM((n_dp, ff // n_dp, d), BF16)
    mixed, d_tokens, d_gates, d_w_down = pl.pallas_call(
        functools.partial(kernel, n, n_dp, cap, scale),
        out_shape=(
            jax.ShapeDtypeStruct((t, d), BF16),
            jax.ShapeDtypeStruct((t, d), BF16),
            jax.ShapeDtypeStruct((1, t), F32),
            jax.ShapeDtypeStruct((1, ff // n_dp, d), BF16),
        ),
        in_specs=[vmem, vmem, vmem, hbm, hbm, hbm, vmem],
        out_specs=(vmem,) * 4,
        scratch_shapes=[block] * 8
        + [part] * 2
        + [
            pltpu.VMEM((d, ff), BF16),
            pltpu.VMEM((d, ff), BF16),
            pltpu.VMEM((ff, d), BF16),
            pltpu.VMEM((t, d), BF16),
            pltpu.SemaphoreType.DMA((4, n)),
            pltpu.SemaphoreType.DMA((4, n)),
            pltpu.SemaphoreType.DMA((n_dp,)),
            pltpu.SemaphoreType.DMA((n_dp,)),
            pltpu.SemaphoreType.DMA((3,)),
        ],
        compiler_params=pltpu.CompilerParams(
            collective_id=0, has_side_effects=True, vmem_limit_bytes=56 * 2**20
        ),
    )(
        tokens, routes.reshape(1, t), route_gates.reshape(1, t),
        w_gate, w_up, w_down, cotangent,
    )
    return mixed, d_tokens, d_gates.reshape(t, 1), d_w_down


def solution(mesh):
    split = P(("dp", "expert"), None)
    weights = P("expert", None, None)
    return jax.shard_map(
        functools.partial(per_device, mesh.shape["expert"], mesh.shape["dp"]),
        mesh=mesh,
        in_specs=(split, split, split, weights, weights, weights, split),
        out_specs=(split, split, split, P("expert", "dp", None)),
        check_vma=False,
    )
```

time: 144 us -> 70.5 us (0.49); the launches traced: 142 us -> 70.3 us
  Pallas kernels: 0 us -> 64.6 us
  blocking collectives: 60.7 us -> 0 us
  waiting for transfers between devices: 33.9 us -> 0 us
  between operations: 14.2 us -> 0.66 us
  matrix products: 8.87 us -> 0 us
  other arithmetic: 7.14 us -> 0 us
  local copies, waits for them, and re-layouts: 11.5 us -> 5 us
  starting transfers between devices: 5.26 us -> 0 us
    pallas_call x0 -> x1, Pallas kernels: none -> 64.6 us  [per_device(): pl.pallas_call(functools.partial(kernel, n, n_dp, cap, scale), out_shape=...]
    all_to_all x3 -> x0, blocking collectives: 60.7 us -> none  [the longest x1 20.7 us: per_device(): lax.all_to_all(outgoing, 'expert', split_axis=0, concat_axis=0, tiled=True)]
    reduce_scatter x1 -> x0, waiting for transfers between devices: 20.7 us -> none  [per_device(): lax.psum_scatter(product * grad_scale, 'dp', scatter_dimension=0, tiled=T...]
    all_to_all x1 -> x0, waiting for transfers between devices: 13.2 us -> none  [send_back(): lax.all_to_all(values, 'expert', split_axis=0, concat_axis=0, tiled=True)]
    dot_general x7 -> x0, matrix products: 8.87 us -> none  [the longest x1 2.26 us: per_device(): lax.dot_general(hidden_rows, grad_rows, (((0,), (0,)), ((), ())), preferr...]
    gather x4 -> x0, local copies, waits for them, and re-layouts: 6.48 us -> none  [the longest x1 2.79 us: per_device(): tokens[source_row // route_count]]
    all_to_all x1 -> x0, starting transfers between devices: 5.26 us -> none  [send_back(): lax.all_to_all(values, 'expert', split_axis=0, concat_axis=0, tiled=True)]
    dot_general x1 -> x0, other arithmetic: 2.68 us -> none  [per_device(): jnp.einsum('td,tkd->tk', cotangent, out_rows, preferred_element_type=jnp....]
  transfers between devices with their start and end apart: 2 -> 0, of which waited for: 2 -> 0; matrix products, arithmetic and copies ran while one was open for 4% -> 0% of each run, Pallas kernels for 0% -> 0%
where the time goes in v1:
time: 70.5 us; the launch traced here: 70.3 us
  Pallas kernels  64.6 us (92%)
  local copies, waits for them, and re-layouts  5 us (7%)
    pallas_call x1, Pallas kernels, per_device(): pl.pallas_call(functools.partial(kernel, n, n_dp, cap, scale), out_shape=...  64.6 us
    unnamed x8, local copies, waits for them, and re-layouts  5 us

profile of v1, /device:TPU:8, one launch (start us, length us, event | category | flops | bytes accessed | tf_op | source)
XLA Modules:
  0.0 70.3 jit_solution(15166716329919793342)
XLA Ops:
  0.6 64.6 %shard_map.102 = (bf16[128,2048]{1,0:T(8,128)(2,1)}, bf16[128,2048]{1,0:T(8,128)(2,1)}, f32[1,128]{1,0:T(1,128)}, bf16[1,48,2048]{2,1,0:T(8,128)(2,1)}) custom-call(bf16[128,2048]{1,0:T(8,128)(2,1)} %tokens.1, s32[1,128]{1,0:T(1,128)} %bitcast.3, f32[1,128]{1,0:T(1,128)} %bitcast.4, bf16[1,2048,384]{2,1,0:T(8,128)(2,1)} %w_gate_hbm.1, ...), custom_call_target="tpu_custom_call" | custom-call | tf_op jit(solution)/shard_map/pallas_call | solution.py:187
  65.3 0.0 copy-start.1
  65.3 0.0 copy-start
  65.3 1.9 %copy.15 = bf16[128,2048]{1,0:T(8,128)(2,1)} copy(bf16[128,2048]{1,0:T(8,128)(2,1)} %get-tuple-element.16) | data formatting | bytes 1048576
  67.2 1.9 %copy.16 = bf16[128,2048]{1,0:T(8,128)(2,1)} copy(bf16[128,2048]{1,0:T(8,128)(2,1)} %get-tuple-element.17) | data formatting | bytes 1048576
  69.1 0.0 copy-done.1
  69.1 0.5 copy.17
  69.6 0.0 copy-done
  69.6 0.7 copy.18
Async XLA Ops:
  65.3 3.8 %copy-start.1 = (f32[1,128]{1,0:T(1,128)S(1)}, f32[1,128]{1,0:T(1,128)}, u32[]{:S(2)}) copy-start(f32[1,128]{1,0:T(1,128)} %get-tuple-element.10) | copy-start | bytes 1540
  65.3 4.3 %copy-start = (bf16[1,48,2048]{2,1,0:T(8,128)(2,1)S(1)}, bf16[1,48,2048]{2,1,0:T(8,128)(2,1)}, u32[]{:S(2)}) copy-start(bf16[1,48,2048]{2,1,0:T(8,128)(2,1)} %get-tuple-element.19) | copy-start | bytes 589828

commit v2 on v1

--- a/solution.py
+++ b/solution.py
@@ -27,16 +27,44 @@
 
 def kernel(
     n, n_dp, cap, scale,
-    tokens, routes, gates, w_gate_hbm, w_up_hbm, w_down_hbm, cotangent,
-    mixed, d_tokens, d_gates, d_w_down,
+    tokens_hbm, routes, gates, w_gate_hbm, w_up_hbm, w_down_hbm, cotangent_hbm,
+    mixed_hbm, d_tokens_hbm, d_gates_hbm, d_w_down_hbm,
+    tokens, cotangent, mixed, d_tokens, d_gates, d_w_down,
     x_send, g_send, out_send, gi_send, x_recv, g_recv, out_recv, gi_recv,
     part_send, part_recv, w_gate, w_up, w_down, weighted,
-    send_sem, recv_sem, part_send_sem, part_recv_sem, weight_sem,
+    send_sem, recv_sem, part_send_sem, part_recv_sem, weight_sem, row_sem, result_sem,
 ):
     me = lax.axis_index("expert")
     my_dp = lax.axis_index("dp")
     t = tokens.shape[0]
 
+    barrier = pltpu.get_barrier_semaphore()
+    for k in range(1, n):
+        pl.semaphore_signal(
+            barrier, inc=1, device_id={"expert": lax.rem(me + k, n)}, device_id_type=MESH
+        )
+    for k in range(1, n_dp):
+        pl.semaphore_signal(
+            barrier, inc=1, device_id={"dp": lax.rem(my_dp + k, n_dp)}, device_id_type=MESH
+        )
+
+    row_copies = [
+        pltpu.make_async_copy(src, dst, row_sem.at[i])
+        for i, (src, dst) in enumerate(((tokens_hbm, tokens), (cotangent_hbm, cotangent)))
+    ]
+    for copy in row_copies:
+        copy.start()
+    results = [
+        pltpu.make_async_copy(src, dst, result_sem.at[i])
+        for i, (src, dst) in enumerate(
+            (
+                (mixed, mixed_hbm),
+                (d_tokens, d_tokens_hbm),
+                (d_gates, d_gates_hbm),
+                (d_w_down, d_w_down_hbm),
+            )
+        )
+    ]
     weight_copies = [
         pltpu.make_async_copy(src.at[0], dst, weight_sem.at[i])
         for i, (src, dst) in enumerate(
@@ -45,16 +73,6 @@
     ]
     for copy in weight_copies:
         copy.start()
-
-    barrier = pltpu.get_barrier_semaphore()
-    for k in range(1, n):
-        pl.semaphore_signal(
-            barrier, inc=1, device_id={"expert": lax.rem(me + k, n)}, device_id_type=MESH
-        )
-    for k in range(1, n_dp):
-        pl.semaphore_signal(
-            barrier, inc=1, device_id={"dp": lax.rem(my_dp + k, n_dp)}, device_id_type=MESH
-        )
 
     row = routes[...].astype(F32)
     first = lax.broadcasted_iota(jnp.int32, (t, t), 0)
@@ -84,6 +102,7 @@
             device_id_type=MESH,
         )
 
+    row_copies[0].wait()
     picks = [pick(lax.rem(me + k, n)) for k in range(n)]
     sends = [[], [], [], []]
     for k in range(1, n):
@@ -92,6 +111,7 @@
             pl.semaphore_wait(barrier, n + n_dp - 2)
         sends[X].append(exchange(X, k, x_send.at[k], x_recv))
         sends[X][-1].start()
+    row_copies[1].wait()
     weighted[...] = (gate_column * cotangent[...].astype(F32)).astype(BF16)
     for k in range(1, n):
         g_send[k] = dot(picks[k], weighted[...]).astype(BF16)
@@ -159,19 +179,39 @@
     mixed[...] = (gate_column * rows).astype(BF16)
     inner = jnp.sum(cotangent[...].astype(F32) * rows, axis=1, keepdims=True)
     d_gates[...] = jnp.sum(jnp.where(eye, inner, 0.0), axis=0, keepdims=True)
+    results[0].start()
+    results[2].start()
 
     total = part_send[my_dp].astype(F32)
     for k, copy in enumerate(parts, 1):
         copy.wait_recv()
         total = total + part_recv[k].astype(F32)
     d_w_down[0] = total.astype(BF16)
+    results[3].start()
 
     for copy in sends[GI]:
         copy.wait_recv()
     d_tokens[...] = dot(spread, joined(gi_recv, n)).astype(BF16)
+    results[1].start()
     for copies in (*sends, parts):
         for copy in copies:
             copy.wait_send()
+    for copy in results:
+        copy.wait()
+
+
+def hand_over(count, *refs):
+    made, results, held = refs[:count], refs[count : 2 * count], refs[2 * count : 3 * count]
+    read_sem, write_sem = refs[3 * count :]
+    reads = [pltpu.make_async_copy(made[i], held[i], read_sem.at[i]) for i in range(count)]
+    writes = [pltpu.make_async_copy(held[i], results[i], write_sem.at[i]) for i in range(count)]
+    for copy in reads:
+        copy.start()
+    for read, write in zip(reads, writes):
+        read.wait()
+        write.start()
+    for copy in writes:
+        copy.wait()
 
 
 def per_device(n, n_dp, tokens, routes, route_gates, w_gate, w_up, w_down, cotangent):
@@ -184,17 +224,21 @@
     hbm = pl.BlockSpec(memory_space=pl.ANY)
     block = pltpu.VMEM((n, cap, d), BF16)
     part = pltpu.VMEM((n_dp, ff // n_dp, d), BF16)
-    mixed, d_tokens, d_gates, d_w_down = pl.pallas_call(
+    shapes = (
+        jax.ShapeDtypeStruct((t, d), BF16),
+        jax.ShapeDtypeStruct((t, d), BF16),
+        jax.ShapeDtypeStruct((1, t), F32),
+        jax.ShapeDtypeStruct((1, ff // n_dp, d), BF16),
+    )
+    made = pl.pallas_call(
         functools.partial(kernel, n, n_dp, cap, scale),
-        out_shape=(
-            jax.ShapeDtypeStruct((t, d), BF16),
-            jax.ShapeDtypeStruct((t, d), BF16),
-            jax.ShapeDtypeStruct((1, t), F32),
-            jax.ShapeDtypeStruct((1, ff // n_dp, d), BF16),
-        ),
-        in_specs=[vmem, vmem, vmem, hbm, hbm, hbm, vmem],
-        out_specs=(vmem,) * 4,
-        scratch_shapes=[block] * 8
+        out_shape=shapes,
+        in_specs=[hbm, vmem, vmem, hbm, hbm, hbm, hbm],
+        out_specs=(hbm,) * 4,
+        scratch_shapes=[
+            pltpu.VMEM(s.shape, s.dtype) for s in (shapes[0], shapes[0], *shapes)
+        ]
+        + [block] * 8
         + [part] * 2
         + [
             pltpu.VMEM((d, ff), BF16),
@@ -206,6 +250,8 @@
             pltpu.SemaphoreType.DMA((n_dp,)),
             pltpu.SemaphoreType.DMA((n_dp,)),
             pltpu.SemaphoreType.DMA((3,)),
+            pltpu.SemaphoreType.DMA((2,)),
+            pltpu.SemaphoreType.DMA((4,)),
         ],
         compiler_params=pltpu.CompilerParams(
             collective_id=0, has_side_effects=True, vmem_limit_bytes=56 * 2**20
@@ -214,6 +260,14 @@
         tokens, routes.reshape(1, t), route_gates.reshape(1, t),
         w_gate, w_up, w_down, cotangent,
     )
+    mixed, d_tokens, d_gates, d_w_down = pl.pallas_call(
+        functools.partial(hand_over, len(shapes)),
+        out_shape=shapes,
+        in_specs=[hbm] * 4,
+        out_specs=(hbm,) * 4,
+        scratch_shapes=[pltpu.VMEM(s.shape, s.dtype) for s in shapes]
+        + [pltpu.SemaphoreType.DMA((len(shapes),))] * 2,
+    )(*made)
     return mixed, d_tokens, d_gates.reshape(t, 1), d_w_down
 
 

time: 70.5 us -> 66.8 us (0.948)
  local copies, waits for them, and re-layouts: 5 us -> 0 us
  Pallas kernels: 64.6 us -> 66 us
    unnamed x8 -> x0, local copies, waits for them, and re-layouts: 5 us -> none
    pallas_call x0 -> x1, Pallas kernels: none -> 2.14 us  [per_device(): pl.pallas_call(functools.partial(hand_over, len(shapes)), out_shape=shape...]
    pallas_call x1, Pallas kernels: 64.6 us -> 63.8 us  [per_device(): pl.pallas_call(functools.partial(kernel, n, n_dp, cap, scale), out_shape=...]
where the time goes in v2:
time: 66.8 us; the launch traced here: 66.6 us
  Pallas kernels  66 us (99%)
    pallas_call x1, Pallas kernels, per_device(): pl.pallas_call(functools.partial(kernel, n, n_dp, cap, scale), out_shape=...  63.8 us
    pallas_call x1, Pallas kernels, per_device(): pl.pallas_call(functools.partial(hand_over, len(shapes)), out_shape=shape...  2.14 us

profile of v2, /device:TPU:8, one launch (start us, length us, event | category | flops | bytes accessed | tf_op | source)
XLA Modules:
  0.0 66.6 jit_solution(3971270179136685805)
XLA Ops:
  0.6 63.8 %shard_map.102 = (bf16[128,2048]{1,0:T(8,128)(2,1)}, bf16[128,2048]{1,0:T(8,128)(2,1)}, f32[1,128]{1,0:T(1,128)}, bf16[1,48,2048]{2,1,0:T(8,128)(2,1)}) custom-call(bf16[128,2048]{1,0:T(8,128)(2,1)} %tokens_hbm.1, s32[1,128]{1,0:T(1,128)} %bitcast.3, f32[1,128]{1,0:T(1,128)} %bitcast.4, bf16[1,2048,384]{2,1,0:T(8,128)(2,1)} %w_gate_hbm.1, ...), custom_call_target="tpu_custom_call" | custom-call | tf_op jit(solution)/shard_map/pallas_call | solution.py:233
  64.5 2.1 %shard_map.103 = (bf16[128,2048]{1,0:T(8,128)(2,1)}, bf16[128,2048]{1,0:T(8,128)(2,1)}, f32[1,128]{1,0:T(1,128)}, bf16[1,48,2048]{2,1,0:T(8,128)(2,1)}) custom-call(bf16[128,2048]{1,0:T(8,128)(2,1)} %get-tuple-element.12.refs_0_, bf16[128,2048]{1,0:T(8,128)(2,1)} %get-tuple-element.13.refs_1_, f32[1,128]{1,0:T(1,128)} %get-tuple-element.14.refs_2_, ...), custom_call_target="tpu_custom_call" | custom-call | tf_op jit(solution)/shard_map/pallas_call | solution.py:263
